TPU v7x, 128 devices: a whole 4x4x4 slice. The times are simulated.
128 devices in a mesh: ctx: 8 (over y, z_lo), tp: 16 (over x, z_hi, core).
Axes of the slice: x: 4, y: 4, z: 4 (z_hi: 2, z_lo: 2; z = z_hi * 2 + z_lo), core: 2. Of those that a mesh axis runs over, the one named last changes fastest.
Arguments:
- context: bfloat16 [16384, 4096], P('ctx', 'tp'), may hold values from -6 to 6
- residual: bfloat16 [16384, 2048], P(('ctx', 'tp')), may hold values from -6 to 6
- o_weight: bfloat16 [4096, 2048], P('tp'), may hold values from -0.09375 to 0.09375
- norm_gain: bfloat16 [2048], replicated, may hold values from 0.099609375 to 1.8984375
- routes: int32 [16384, 4], P(('ctx', 'tp')), may hold values from 0 to 127, all different within a row; in each aligned block of 128 rows (0 to 127, 128 to 255, ...) at most 6 rows name the same one
- gate_weights: float32 [16384, 4], P(('ctx', 'tp')), may hold values from 0.05 to 0.5
- expert_in: bfloat16 [128, 2048, 1536], P(('ctx', 'tp')), may hold values from -0.125 to 0.125
- expert_out: bfloat16 [128, 768, 2048], P(('ctx', 'tp')), may hold values from -0.21875 to 0.21875
- cotangent: bfloat16 [16384, 2048], P(('ctx', 'tp')), may hold values from -6 to 6
Outputs:
- layer_out: bfloat16 [16384, 2048], P(('ctx', 'tp'))
- d_context: bfloat16 [16384, 4096], P('ctx', 'tp')
- d_residual: bfloat16 [16384, 2048], P(('ctx', 'tp'))
- d_o_weight: float32 [4096, 2048], P('tp', 'ctx')
- d_gain: float32 [2048], replicated
- d_expert_in: bfloat16 [128, 2048, 1536], P(('ctx', 'tp'))
- d_expert_out: bfloat16 [128, 768, 2048], P(('ctx', 'tp'))
Inputs may be any that keep to these rules, and one draw needn't show every extreme that they name: `routes`: each token names 4 different experts; the 128 tokens of one device (aligned blocks) name one expert at most 6 times, a bound that some block reaches.
All inputs are finite; a program needn't handle non-finite values.
Results may differ from a plain program's by a relative error of at most 0.019.
Values may be sent and summed in bfloat16 or wider, within the bound.
No kernel may reach another device: no remote copies, remote signals or barrier semaphores. Data moves between devices by JAX's collectives and lax.ppermute only.
A program may use at most 128 MiB of HBM per device.

v0:
```python
import jax
import jax.numpy as jnp
from jax import lax
from jax.sharding import PartitionSpec as P


def contract(left_arr, right_arr, left_dim, right_dim):
    return lax.dot_general(
        left_arr,
        right_arr,
        (((left_dim,), (right_dim,)), ((), ())),
        preferred_element_type=jnp.float32,
    )


def trade_rows(buffer, n_ctx, n_tp, capacity):
    model_width = buffer.shape[1]
    shaped = buffer.reshape(n_ctx * n_tp, capacity, model_width)
    moved = lax.all_to_all(shaped, ("ctx", "tp"), split_axis=0, concat_axis=0, tiled=True)
    return moved.reshape(n_ctx * n_tp * capacity, model_width)


def on_device(
    context, residual, o_weight, norm_gain, routes, gate_weights, expert_in, expert_out, cotangent
):
    tok_rows, model_width = residual.shape
    n_tp = lax.axis_size("tp")
    n_ctx = lax.axis_size("ctx")
    n_all = n_tp * n_ctx
    route_count = routes.shape[1]
    capacity = max(2, 3 * tok_rows * route_count // (2 * n_all))
    ctx_rows = context
    attention = lax.psum_scatter(
        jnp.dot(ctx_rows, o_weight, preferred_element_type=jnp.float32),
        "tp",
        scatter_dimension=0,
        tiled=True,
    )
    mixed = (residual.astype(jnp.float32) + attention).astype(jnp.bfloat16)
    mixed_f = mixed.astype(jnp.float32)
    inv_rms = lax.rsqrt(jnp.mean(mixed_f * mixed_f, axis=-1, keepdims=True) + 1e-06)
    normed = mixed_f * inv_rms
    gain_f = norm_gain.astype(jnp.float32)
    normed_h = (normed * gain_f).astype(jnp.bfloat16)
    route_ids = routes.reshape(-1)
    expert_iota = jnp.arange(n_all, dtype=jnp.int32)
    one_hot = (route_ids[:, None] == expert_iota[None, :]).astype(jnp.int32)
    route_rank = jnp.cumsum(one_hot, axis=0) - one_hot
    slot_ids = jnp.sum(route_rank * one_hot, axis=-1)
    targets = route_ids * capacity + slot_ids

    def to_slots(values):
        empty = jnp.zeros((n_all * capacity, model_width), jnp.bfloat16)
        return empty.at[targets].set(values)

    h_routes = jnp.broadcast_to(normed_h[:, None, :], (tok_rows, route_count, model_width))
    arrived = trade_rows(to_slots(h_routes.reshape(-1, model_width)), n_ctx, n_tp, capacity)
    weight_in = expert_in[0]
    weight_out = expert_out[0]
    hidden = weight_out.shape[0]
    gate_up = jnp.dot(arrived, weight_in, preferred_element_type=jnp.float32)
    gate_part = gate_up[:, :hidden]
    up_part = gate_up[:, hidden:]
    sigma = jax.nn.sigmoid(gate_part)
    act = (gate_part * sigma * up_part).astype(jnp.bfloat16)
    expert_y = jnp.dot(act, weight_out, preferred_element_type=jnp.float32).astype(jnp.bfloat16)
    returned = trade_rows(expert_y, n_ctx, n_tp, capacity)
    picked = returned[targets].reshape(tok_rows, route_count, model_width).astype(jnp.float32)
    moe_sum = jnp.sum(picked * gate_weights[:, :, None], axis=1)
    layer_out = (mixed_f + moe_sum).astype(jnp.bfloat16)
    cot_f = cotangent.astype(jnp.float32)
    grad_y = (gate_weights[:, :, None] * cot_f[:, None, :]).astype(jnp.bfloat16)
    grads = trade_rows(to_slots(grad_y.reshape(-1, model_width)), n_ctx, n_tp, capacity)
    grad_act = contract(grads, weight_out, 1, 1)
    grad_gate = grad_act * up_part * sigma * (1.0 + gate_part * (1.0 - sigma))
    grad_up = grad_act * gate_part * sigma
    grad_gate_up = jnp.concatenate([grad_gate, grad_up], axis=1).astype(jnp.bfloat16)
    d_expert_out = contract(act, grads, 0, 0).astype(jnp.bfloat16)[None]
    d_expert_in = contract(arrived, grad_gate_up, 0, 0).astype(jnp.bfloat16)[None]
    grad_route = contract(grad_gate_up, weight_in, 1, 1).astype(jnp.bfloat16)
    grad_back = trade_rows(grad_route, n_ctx, n_tp, capacity)
    grad_h = jnp.sum(
        grad_back[targets].reshape(tok_rows, route_count, model_width).astype(jnp.float32), axis=1
    )
    d_gain = lax.psum(jnp.sum(grad_h * normed, axis=0), ("ctx", "tp"))
    grad_n = grad_h * gain_f
    inner = jnp.mean(grad_n * normed, axis=-1, keepdims=True)
    d_residual = (cot_f + inv_rms * (grad_n - normed * inner)).astype(jnp.bfloat16)
    shard_rows = lax.all_gather(d_residual, "tp", axis=0, tiled=True)
    ctx_rows = context
    weight_grad = contract(ctx_rows, shard_rows, 0, 0)
    rows_grad = contract(shard_rows, o_weight, 1, 1)
    ctx_grad = rows_grad
    ctx_grad, weight_grad = (ctx_grad, weight_grad)
    d_context = ctx_grad.astype(jnp.bfloat16)
    d_o_weight = lax.psum_scatter(
        weight_grad.astype(jnp.bfloat16), "ctx", scatter_dimension=1, tiled=True
    ).astype(jnp.float32)
    return (layer_out, d_context, d_residual, d_o_weight, d_gain, d_expert_in, d_expert_out)


def solution(mesh):
    in_specs = (
        P("ctx", "tp"),
        P(("ctx", "tp"), None),
        P("tp", None),
        P(),
        P(("ctx", "tp"), None),
        P(("ctx", "tp"), None),
        P(("ctx", "tp"), None, None),
        P(("ctx", "tp"), None, None),
        P(("ctx", "tp"), None),
    )
    out_specs = (
        P(("ctx", "tp"), None),
        P("ctx", "tp"),
        P(("ctx", "tp"), None),
        P("tp", "ctx"),
        P(),
        P(("ctx", "tp"), None, None),
        P(("ctx", "tp"), None, None),
    )
    return jax.shard_map(
        on_device, mesh=mesh, in_specs=in_specs, out_specs=out_specs, check_vma=False
    )
```

profile of v0, /device:TPU:2, one launch (start us, length us, event | category | flops | bytes accessed | tf_op | source)
XLA Modules:
  0.0 629.0 jit_solution(12848908958714409118)
XLA Ops:
  7.2 9.8 %fusion.38 = f32[2048,2048]{1,0:T(8,128)} fusion(bf16[2048,256]{1,0:T(8,128)(2,1)} %param.9, bf16[256,2048]{1,0:T(8,128)(2,1)} %param.11), kind=kOutput, calls=%fused_computation.66 | convolution fusion | flops 2147483648 | bytes 18874368 | tf_op jit(solution)/shard_map/dot_general | solution.py:34
  17.0 0.7 copy-done.10
  18.9 4.2 mul.129
  23.1 5.3 mul.130
  28.7 8.3 %scatter_custom_fusion.1 = bf16[768,2048]{1,0:T(8,128)(2,1)} fusion(s32[512]{0:T(512)S(1)} %bitcast.51, f32[512,2048]{1,0:T(8,128)} %mul.130, f32[512]{0:T(512)S(1)} %mul.127, bf16[]{:T(256)} %constant.8.clone.1), kind=kCustom, calls=%fused_computation.27 | custom fusion | flops 2097152 | bytes 7342082 | tf_op jit(solution)/shard_map/scatter | solution.py:54
  37.0 6.7 %reshape.118 = bf16[128,6,2048]{2,1,0:T(8,128)(2,1)} reshape(bf16[768,2048]{1,0:T(8,128)(2,1)} %scatter_custom_fusion.1) | data formatting | bytes 6291456 | tf_op jit(solution)/shard_map/reshape | solution.py:18
  43.6 11.9 %all-to-all-start.2 = ((bf16[128,6,2048]{2,1,0:T(8,128)(2,1)}), bf16[128,6,2048]{2,1,0:T(8,128)(2,1)}, u32[]{:S(2)}, u32[]{:S(2)}) async-start(bf16[128,6,2048]{2,1,0:T(8,128)(2,1)} %reshape.118), calls=%async_computation.3 | async-start | bytes 8388608 | tf_op jit(solution)/shard_map/all_to_all | solution.py:19
  55.6 155.9 %reduce-scatter.3.cloned.1.call-done = f32[128,2048]{1,0:T(8,128)} async-done(((f32[2048,2048]{1,0:T(8,128)}), f32[128,2048]{1,0:T(8,128)}) %reduce-scatter.3.cloned.1.call-update) | async-done | bytes 1048592 | tf_op jit(solution)/shard_map/reduce_scatter | solution.py:33
  211.5 1.6 fusion.29
  213.1 0.8 copy-done.4
  214.1 2.4 broadcast_in_dim.6
  216.5 3.9 reshape.144
  220.4 6.7 %scatter_custom_fusion = bf16[768,2048]{1,0:T(8,128)(2,1)} fusion(s32[512]{0:T(512)S(1)} %bitcast.52, bf16[512,2048]{1,0:T(8,128)(2,1)} %reshape.144, bf16[]{:T(256)} %constant.8.clone.1), kind=kCustom, calls=%fused_computation.30 | custom fusion | bytes 3146240 | tf_op jit(solution)/shard_map/scatter | solution.py:54
  227.2 6.2 reshape.114
  233.4 7.8 %all-to-all-start = ((bf16[128,6,2048]{2,1,0:T(8,128)(2,1)}), bf16[128,6,2048]{2,1,0:T(8,128)(2,1)}, u32[]{:S(2)}, u32[]{:S(2)}) async-start(bf16[128,6,2048]{2,1,0:T(8,128)(2,1)} %reshape.114), calls=%async_computation.1 | async-start | bytes 8388608 | tf_op jit(solution)/shard_map/all_to_all | solution.py:19
  241.2 6.3 %reshape.119 = bf16[768,2048]{1,0:T(8,128)(2,1)} reshape(bf16[128,6,2048]{2,1,0:T(8,128)(2,1)} %all-to-all-done.2) | data formatting | bytes 6291456 | tf_op jit(solution)/shard_map/reshape | solution.py:20
  247.6 45.5 %all-to-all-done = bf16[128,6,2048]{2,1,0:T(8,128)(2,1)} async-done(((bf16[128,6,2048]{2,1,0:T(8,128)(2,1)}), bf16[128,6,2048]{2,1,0:T(8,128)(2,1)}, u32[]{:S(2)}, u32[]{:S(2)}) %all-to-all-start) | async-done | bytes 3145760 | tf_op jit(solution)/shard_map/all_to_all | solution.py:19
  293.1 6.3 %reshape.115 = bf16[768,2048]{1,0:T(8,128)(2,1)} reshape(bf16[128,6,2048]{2,1,0:T(8,128)(2,1)} %all-to-all-done) | data formatting | bytes 6291456 | tf_op jit(solution)/shard_map/reshape | solution.py:20
  299.4 8.2 %fusion.3 = f32[768,1536]{1,0:T(8,128)S(1)} fusion(bf16[768,2048]{1,0:T(8,128)(2,1)} %reshape.115, bf16[1,2048,1536]{2,1,0:T(8,128)(2,1)} %param.15), kind=kOutput, calls=%fused_computation.8 | convolution fusion | flops 4831838208 | bytes 14155776 | tf_op jit(solution)/shard_map/dot_general | solution.py:61
  307.7 4.5 multiply_convert_fusion.2
  312.2 1.0 copy-done.13
  313.2 0.4 copy-done.14
  313.6 6.4 %fusion.5 = bf16[768,2048]{1,0:T(8,128)(2,1)} fusion(bf16[1,2048,1536]{2,1,0:T(8,128)(2,1)S(1)} %bitcast.55, bf16[768,768]{1,0:T(8,128)(2,1)S(1)} %get-tuple-element.26, bf16[768,768]{1,0:T(8,128)(2,1)S(1)} %get-tuple-element.25), kind=kOutput, calls=%fused_computation.14 | convolution fusion | flops 4838129664 | bytes 11796480 | tf_op jit(solution)/shard_map/dot_general | solution.py:8
  320.0 6.2 reshape.120
  326.2 6.5 %all-to-all-start.3 = ((bf16[128,6,2048]{2,1,0:T(8,128)(2,1)}), bf16[128,6,2048]{2,1,0:T(8,128)(2,1)}, u32[]{:S(2)}, u32[]{:S(2)}) async-start(bf16[128,6,2048]{2,1,0:T(8,128)(2,1)} %reshape.120), calls=%async_computation.4 | async-start | bytes 8388608 | tf_op jit(solution)/shard_map/all_to_all | solution.py:19
  332.8 5.2 convolution_convert_fusion.2
  338.0 6.2 reshape.116
  344.2 40.3 %all-to-all-done.3 = bf16[128,6,2048]{2,1,0:T(8,128)(2,1)} async-done(((bf16[128,6,2048]{2,1,0:T(8,128)(2,1)}), bf16[128,6,2048]{2,1,0:T(8,128)(2,1)}, u32[]{:S(2)}, u32[]{:S(2)}) %all-to-all-start.3) | async-done | bytes 3145760 | tf_op jit(solution)/shard_map/all_to_all | solution.py:19
  384.5 6.8 %all-to-all-start.1 = ((bf16[128,6,2048]{2,1,0:T(8,128)(2,1)}), bf16[128,6,2048]{2,1,0:T(8,128)(2,1)}, u32[]{:S(2)}, u32[]{:S(2)}) async-start(bf16[128,6,2048]{2,1,0:T(8,128)(2,1)} %reshape.116), calls=%async_computation.2 | async-start | bytes 8388608 | tf_op jit(solution)/shard_map/all_to_all | solution.py:19
  391.6 4.9 reshape.121
  396.5 3.3 gather_fusion.1
  399.8 4.7 reshape.123
  404.5 4.9 reduce_sum.60
  409.4 0.4 fusion.28
  409.8 0.6 copy-done.2
  410.4 32.7 %all-to-all-done.1 = bf16[128,6,2048]{2,1,0:T(8,128)(2,1)} async-done(((bf16[128,6,2048]{2,1,0:T(8,128)(2,1)}), bf16[128,6,2048]{2,1,0:T(8,128)(2,1)}, u32[]{:S(2)}, u32[]{:S(2)}) %all-to-all-start.1) | async-done | bytes 3145760 | tf_op jit(solution)/shard_map/all_to_all | solution.py:19
  443.1 4.9 reshape.117
  448.0 3.3 gather_fusion
  451.2 4.7 reshape.122
  456.0 5.5 multiply_reduce_fusion
  461.5 1.4 fusion.27
  463.2 6.6 %fusion.11 = bf16[1,768,2048]{2,1,0:T(8,128)(2,1)} fusion(bf16[768,768]{1,0:T(8,128)(2,1)} %get-tuple-element.27, bf16[768,2048]{1,0:T(8,128)(2,1)} %reshape.119), kind=kOutput, calls=%fused_computation.18 | convolution fusion | flops 2417491968 | bytes 7471104 | tf_op jit(solution)/shard_map/dot_general | solution.py:8
  469.8 62.9 %all-gather.2.cloned.1.call-done = bf16[2048,2048]{1,0:T(8,128)(2,1)} async-done(((bf16[128,2048]{1,0:T(8,128)(2,1)}), bf16[2048,2048]{1,0:T(8,128)(2,1)}) %all-gather.2.cloned.1.call-update) | async-done | bytes 8388624 | tf_op jit(solution)/shard_map/all_gather | solution.py:89
  532.7 7.2 %fusion.12 = bf16[256,2048]{0,1:T(8,128)(2,1)} fusion(bf16[2048,2048]{1,0:T(8,128)(2,1)} %all-gather.2.cloned.1.call-done, bf16[2048,256]{1,0:T(8,128)(2,1)} %param.9), kind=kOutput, calls=%fused_computation.21 | convolution fusion | flops 2148007936 | bytes 10485760 | tf_op jit(solution)/shard_map/dot_general | solution.py:8
  539.9 8.6 %fusion = bf16[1,2048,1536]{2,1,0:T(8,128)(2,1)} fusion(bf16[768,2048]{1,0:T(8,128)(2,1)S(1)} %copy-done.7, bf16[768,768]{1,0:T(8,128)(2,1)} %copy-done.14, bf16[768,768]{1,0:T(8,128)(2,1)} %copy-done.13), kind=kOutput, calls=%fused_computation.5 | convolution fusion | flops 4839702528 | bytes 11796480 | tf_op jit(solution)/shard_map/dot_general | solution.py:8
  548.6 64.6 %psum.7 = f32[2048]{0:T(1024)} all-reduce(f32[2048]{0:T(1024)S(1)} %get-tuple-element.21), channel_id=1, replica_groups=mesh['ctx'=8,'tp'=16] {'ctx','tp'}, use_global_device_ids=true, to_apply=%region_12.13 | all-reduce | flops 2048 | bytes 16384 | tf_op jit(solution)/shard_map/psum | solution.py:85
  613.2 7.1 %convolution_convert_fusion.4 = bf16[2048,256]{1,0:T(8,128)(2,1)} fusion(bf16[2048,2048]{1,0:T(8,128)(2,1)} %all-gather.2.cloned.1.call-done, bf16[256,2048]{1,0:T(8,128)(2,1)} %param.11), kind=kOutput, calls=%fused_computation.20 | convolution fusion | flops 2148007936 | bytes 10485760 | tf_op jit(solution)/shard_map/dot_general | solution.py:8
  620.3 1.7 copy.29
  (61 shorter events, 2.3 us)
Async XLA Ops:
  7.2 300.5 %copy-start = (bf16[1,768,2048]{2,1,0:T(8,128)(2,1)S(1)}, bf16[1,768,2048]{2,1,0:T(8,128)(2,1)}, u32[]{:S(2)}) copy-start(bf16[1,768,2048]{2,1,0:T(8,128)(2,1)} %param.16) | copy-start | bytes 9437188
  7.2 204.3 %reduce-scatter.3.cloned.1.call-start = ((), (), s32[]{:S(2)}) async-start(), calls=%async_computation.6 | async-start | bytes 17825792 | tf_op jit(solution)/shard_map/reduce_scatter | solution.py:33
  17.0 0.7 copy-start.10
  17.0 1.7 copy-start.12
  43.6 12.0 %copy-start.11 = (bf16[2048]{0:T(1024)(128)(2,1)S(1)}, bf16[2048]{0:T(1024)(128)(2,1)}, u32[]{:S(2)}) copy-start(bf16[2048]{0:T(1024)(128)(2,1)} %param.12) | copy-start | bytes 12292
  43.6 189.8 %all-to-all-start.2 = ((bf16[128,6,2048]{2,1,0:T(8,128)(2,1)}), bf16[128,6,2048]{2,1,0:T(8,128)(2,1)}, u32[]{:S(2)}, u32[]{:S(2)}) async-start(bf16[128,6,2048]{2,1,0:T(8,128)(2,1)} %reshape.118), calls=%async_computation.3 | async-start | bytes 8388608 | tf_op jit(solution)/shard_map/all_to_all | solution.py:19
  213.1 0.8 copy-start.4
  233.4 59.7 %all-to-all-start = ((bf16[128,6,2048]{2,1,0:T(8,128)(2,1)}), bf16[128,6,2048]{2,1,0:T(8,128)(2,1)}, u32[]{:S(2)}, u32[]{:S(2)}) async-start(bf16[128,6,2048]{2,1,0:T(8,128)(2,1)} %reshape.114), calls=%async_computation.1 | async-start | bytes 8388608 | tf_op jit(solution)/shard_map/all_to_all | solution.py:19
  299.4 8.2 %copy-start.8 = (bf16[768,2048]{1,0:T(8,128)(2,1)S(1)}, bf16[768,2048]{1,0:T(8,128)(2,1)}, u32[]{:S(2)}) copy-start(bf16[768,2048]{1,0:T(8,128)(2,1)} %reshape.119) | copy-start | bytes 9437188
  299.4 14.1 %slice-start = ((s8[6291456]{0:T(1024)(128)(4,1)}), s8[4194304]{0:T(1024)(128)(4,1)S(1)}, s32[]{:S(2)}) async-start(s8[6291456]{0:T(1024)(128)(4,1)} %bitcast.54), calls=%async_computation.9 | async-start | bytes 8388608
  307.7 5.9 slice-start.1
  312.2 1.0 copy-start.13
  312.2 1.4 copy-start.14
  326.2 58.3 %all-to-all-start.3 = ((bf16[128,6,2048]{2,1,0:T(8,128)(2,1)}), bf16[128,6,2048]{2,1,0:T(8,128)(2,1)}, u32[]{:S(2)}, u32[]{:S(2)}) async-start(bf16[128,6,2048]{2,1,0:T(8,128)(2,1)} %reshape.120), calls=%async_computation.4 | async-start | bytes 8388608 | tf_op jit(solution)/shard_map/all_to_all | solution.py:19
  384.5 58.5 %all-to-all-start.1 = ((bf16[128,6,2048]{2,1,0:T(8,128)(2,1)}), bf16[128,6,2048]{2,1,0:T(8,128)(2,1)}, u32[]{:S(2)}, u32[]{:S(2)}) async-start(bf16[128,6,2048]{2,1,0:T(8,128)(2,1)} %reshape.116), calls=%async_computation.2 | async-start | bytes 8388608 | tf_op jit(solution)/shard_map/all_to_all | solution.py:19
  391.3 141.4 %all-gather.2.cloned.1.call-start = ((), (), s32[]{:S(2)}) async-start(), calls=%async_computation.7 | async-start | bytes 8912896 | tf_op jit(solution)/shard_map/all_gather | solution.py:89
  404.5 4.9 copy-start.5
  409.4 1.0 copy-start.2
  456.0 5.5 copy-start.3
  456.0 5.5 copy-start.6
  456.0 5.5 copy-start.9
  462.9 157.4 %reduce-scatter.5.cloned.1.call-start = ((), (), s32[]{:S(2)}) async-start(), calls=%async_computation.8 | async-start | bytes 1179648 | tf_op jit(solution)/shard_map/reduce_scatter | solution.py:96
  469.8 70.1 %copy-start.7 = (bf16[768,2048]{1,0:T(8,128)(2,1)S(1)}, bf16[768,2048]{1,0:T(8,128)(2,1)}, u32[]{:S(2)}) copy-start(bf16[768,2048]{1,0:T(8,128)(2,1)} %reshape.115) | copy-start | bytes 9437188
  613.2 8.8 %copy-start.1 = (bf16[1,768,2048]{2,1,0:T(8,128)(2,1)S(1)}, bf16[1,768,2048]{2,1,0:T(8,128)(2,1)}, u32[]{:S(2)}) copy-start(bf16[1,768,2048]{2,1,0:T(8,128)(2,1)} %param.16) | copy-start | bytes 9437188
Sparse Core Ops, SparseCore 0:
  17.1 194.3 reduce-scatter.2
  463.1 69.6 all-gather.1
  540.0 39.1 reduce-scatter.4
where the time goes:
time: 640 us; the launch traced here: 629 us
  waiting for transfers between devices  337 us (53%)
  local copies, waits for them, and re-layouts  92.4 us (14%)
  blocking collectives  64.6 us (10%)
  matrix products  63.6 us (10%)
  starting transfers between devices  33.7 us (5%)
  other arithmetic  22.8 us (4%)
  between operations  14.5 us (2%)
    reduce_scatter x1, waiting for transfers between devices, on_device(): lax.psum_scatter(jnp.dot(ctx_rows, o_weight, preferred_element_type=jnp.f...  156 us
    all_to_all x4, waiting for transfers between devices, trade_rows(): lax.all_to_all(shaped, ('ctx', 'tp'), split_axis=0, concat_axis=0, tiled=...  119 us
    psum x1, blocking collectives, on_device(): d_gain = lax.psum(jnp.sum(grad_h * normed, axis=0), ('ctx', 'tp'))  64.6 us
    all_gather x1, waiting for transfers between devices, on_device(): shard_rows = lax.all_gather(d_residual, 'tp', axis=0, tiled=True)  62.9 us
    dot_general x6, matrix products, contract(): lax.dot_general(left_arr, right_arr, (((left_dim,), (right_dim,)), ((), (...  40.4 us
    all_to_all x4, starting transfers between devices, trade_rows(): lax.all_to_all(shaped, ('ctx', 'tp'), split_axis=0, concat_axis=0, tiled=...  33.1 us
    reshape x4, local copies, waits for them, and re-layouts, trade_rows(): shaped = buffer.reshape(n_ctx * n_tp, capacity, model_width)  25.4 us
    reshape x4, local copies, waits for them, and re-layouts, trade_rows(): return moved.reshape(n_ctx * n_tp * capacity, model_width)  22.4 us
  transfers between devices with their start and end apart: 7, of which 5 were waited for; matrix products, arithmetic and copies ran while one was open for 17% of the time, Pallas kernels for 0%

commit v1 on v0

v1 whole, which is shorter than its diff:
```python
import functools

import jax
import jax.numpy as jnp
from jax import lax
from jax.experimental import pallas as pl
from jax.experimental.pallas import tpu as pltpu
from jax.sharding import PartitionSpec as P

BF = jnp.bfloat16
F32 = jnp.float32
SLOTS = 6
GROUP = 8
PACK = 3
VMEM = 56 * 1024 * 1024


def mm(a, b, da=1, db=0):
    return lax.dot_general(a, b, (((da,), (db,)), ((), ())), preferred_element_type=F32)


def contract(left_arr, right_arr, left_dim, right_dim):
    return mm(left_arr, right_arr, left_dim, right_dim)


def iota(shape, dim):
    return lax.broadcasted_iota(jnp.int32, shape, dim)


def call(body, name, out, grid, in_specs, out_specs, scratch=(), flops=0, nbytes=0):
    return pl.pallas_call(
        body,
        out_shape=out,
        grid_spec=pltpu.PrefetchScalarGridSpec(
            num_scalar_prefetch=0,
            grid=grid,
            in_specs=in_specs,
            out_specs=out_specs,
            scratch_shapes=scratch,
        ),
        compiler_params=pltpu.CompilerParams(
            dimension_semantics=("arbitrary",) * len(grid), vmem_limit_bytes=VMEM
        ),
        cost_estimate=pl.CostEstimate(flops=flops, bytes_accessed=nbytes, transcendentals=0),
        name=name,
    )


def whole(shape):
    n = len(shape)
    return pl.BlockSpec(shape, lambda i: (0,) * n)


def sds(shape, dtype):
    return jax.ShapeDtypeStruct(shape, dtype)


def slot_table(routes, n_exp):
    rows = routes.shape[0]
    lane = iota((rows, n_exp), 1)
    named = jnp.zeros((rows, n_exp), F32)
    for k in range(routes.shape[1]):
        named = named + (routes[:, k : k + 1] == lane).astype(F32)
    before = (iota((rows, rows), 0) > iota((rows, rows), 1)).astype(BF)
    rank = mm(before, named.astype(BF))
    return jnp.where(named > 0, rank, -1.0)


def gate_table(routes, gates, n_exp):
    rows = routes.shape[0]
    lane = iota((rows, n_exp), 1)
    table = jnp.zeros((rows, n_exp), F32)
    for k in range(routes.shape[1]):
        table = table + jnp.where(routes[:, k : k + 1] == lane, gates[:, k : k + 1], 0.0)
    return table


def thirds(values):
    high = values.astype(BF)
    rest = values - high.astype(F32)
    middle = rest.astype(BF)
    low = (rest - middle.astype(F32)).astype(BF)
    return high, middle, low


def pick_rows(slot, first, count):
    rows, n_exp = slot.shape
    row = iota((count, n_exp), 0) + first
    spread = (row // GROUP == iota((count, n_exp), 1)).astype(BF)
    at = mm(spread, slot.astype(BF), 1, 1)
    place = (iota((count, rows), 0) % GROUP).astype(F32)
    main = (at == place) & (place < SLOTS)
    tails = [(at == (place - SLOTS) * PACK + c) & (place >= SLOTS) for c in range(PACK)]
    return spread, main, tails


def pack_tokens(values, main, tails, quarter):
    out = []
    last = values[:, PACK * quarter :]
    for c in range(PACK):
        pick = jnp.concatenate([main.astype(BF), tails[c].astype(BF)], axis=1)
        source = jnp.concatenate([values[:, c * quarter : (c + 1) * quarter], last], axis=0)
        out.append(mm(pick, source))
    return out


def block_perm(count):
    real = count * SLOTS // GROUP
    row, col = iota((real, count), 0), iota((real, count), 1)
    owner, slot = row // SLOTS, row % SLOTS
    same = owner == col // GROUP
    place = col % GROUP
    main = same & (place == slot)
    tails = [
        same & (place == SLOTS + slot // PACK) & (slot % PACK == c) for c in range(PACK)
    ]
    return main.astype(BF), [t.astype(BF) for t in tails]


def unpack(packed, perm, quarter):
    main, tails = perm
    head = mm(main, packed).astype(BF)
    stack = jnp.concatenate([packed[:, c * quarter : (c + 1) * quarter] for c in range(PACK)], axis=0)
    tail = mm(jnp.concatenate(tails, axis=1), stack).astype(BF)
    return jnp.concatenate([head, tail], axis=1)


def repack(rows, perm, quarter):
    main, tails = perm
    last = rows[:, PACK * quarter :]
    out = []
    for c in range(PACK):
        pick = jnp.concatenate([main, tails[c]], axis=0)
        source = jnp.concatenate([rows[:, c * quarter : (c + 1) * quarter], last], axis=0)
        out.append(mm(pick, source, 0, 0).astype(BF))
    return jnp.concatenate(out, axis=1)


def pack_grads_body(n_exp, rows, routes, gates, cot, out, slot, high, middle, low):
    i = pl.program_id(0)

    @pl.when(i == 0)
    def _():
        slot[...] = slot_table(routes[...], n_exp)
        high[...], middle[...], low[...] = thirds(gate_table(routes[...], gates[...], n_exp))

    quarter = cot.shape[1] // 4
    spread, main, tails = pick_rows(slot[...], i * rows, rows)
    gate = (mm(spread, high[...], 1, 1) + mm(spread, middle[...], 1, 1)) + mm(spread, low[...], 1, 1)
    parts = pack_tokens(cot[...], main, tails, quarter)
    for c in range(PACK):
        own = jnp.sum(jnp.where(main | tails[c], gate, 0.0), axis=1, keepdims=True)
        out[:, c * quarter : (c + 1) * quarter] = (parts[c] * own).astype(BF)


def pack_grads(routes, gates, cot, n_exp):
    tok, width = cot.shape
    total, steps = n_exp * GROUP, 4
    rows = total // steps
    table = pltpu.VMEM((tok, n_exp), BF)
    return call(
        functools.partial(pack_grads_body, n_exp, rows),
        "pack_grads",
        sds((total, width * 3 // 4), BF),
        (steps,),
        [whole(routes.shape), whole(gates.shape), whole(cot.shape)],
        pl.BlockSpec((rows, width * 3 // 4), lambda i: (i, 0)),
        [pltpu.VMEM((tok, n_exp), F32), table, table, table],
        flops=2 * total * 2 * tok * width,
        nbytes=8 * total * width,
    )(routes, gates, cot)


def norm_pack_body(n_exp, rows, routes, parts, residual, gain, out, mixed_out, slot, normed_h):
    i = pl.program_id(0)

    @pl.when(i == 0)
    def _():
        slot[...] = slot_table(routes[...], n_exp)
        tok = residual.shape[0]
        step = 32

        def norm(j, carry):
            at = pl.ds(pl.multiple_of(j * step, step), step)
            total = parts[0, at, :].astype(F32)
            for b in range(1, parts.shape[0]):
                total = total + parts[b, at, :].astype(F32)
            mixed = (residual[at, :].astype(F32) + total).astype(BF)
            mixed_out[at, :] = mixed
            mixed = mixed.astype(F32)
            inv_rms = lax.rsqrt(jnp.mean(mixed * mixed, axis=-1, keepdims=True) + 1e-06)
            normed_h[at, :] = (mixed * inv_rms * gain[...].astype(F32)).astype(BF)
            return carry

        lax.fori_loop(0, tok // step, norm, 0)

    quarter = residual.shape[1] // 4
    _, main, tails = pick_rows(slot[...], i * rows, rows)
    packed = pack_tokens(normed_h[...], main, tails, quarter)
    for c in range(PACK):
        out[:, c * quarter : (c + 1) * quarter] = packed[c].astype(BF)


def norm_pack(routes, parts, residual, gain, n_exp):
    tok, width = residual.shape
    total, steps = n_exp * GROUP, 4
    rows = total // steps
    return call(
        functools.partial(norm_pack_body, n_exp, rows),
        "norm_pack",
        (sds((total, width * 3 // 4), BF), sds((tok, width), BF)),
        (steps,),
        [whole(routes.shape), whole(parts.shape), whole(residual.shape), whole(gain.shape)],
        (pl.BlockSpec((rows, width * 3 // 4), lambda i: (i, 0)), whole((tok, width))),
        [pltpu.VMEM((tok, n_exp), F32), pltpu.VMEM((tok, width), BF)],
        flops=2 * total * 2 * tok * width,
        nbytes=16 * total * width,
    )(routes, parts, residual, gain)


def pick_tokens(slot):
    rows, n_exp = slot.shape
    total = n_exp * GROUP
    spread = (iota((n_exp, total), 1) // GROUP == iota((n_exp, total), 0)).astype(BF)
    at = mm(slot.astype(BF), spread)
    place = (iota((rows, total), 1) % GROUP).astype(F32)
    main = (at == place) & (place < SLOTS)
    tails = [(at == (place - SLOTS) * PACK + c) & (place >= SLOTS) for c in range(PACK)]
    return spread, main, tails


def combine_grads_body(n_exp, routes, packed, mixed_ref, gain, cot, out, gain_out):
    tok, width = cot.shape
    quarter = width // 4
    _, main, tails = pick_tokens(slot_table(routes[...], n_exp))
    heads, last = [], jnp.zeros((tok, quarter), F32)
    for c in range(PACK):
        pick = jnp.concatenate([main.astype(BF), tails[c].astype(BF)], axis=0)
        both = mm(pick, packed[:, c * quarter : (c + 1) * quarter])
        heads.append(both[:tok])
        last = last + both[tok:]
    grad_h = jnp.concatenate(heads + [last], axis=1)
    mixed = mixed_ref[...].astype(F32)
    inv_rms = lax.rsqrt(jnp.mean(mixed * mixed, axis=-1, keepdims=True) + 1e-06)
    normed = mixed * inv_rms
    d_gain = jnp.sum(grad_h * normed, axis=0, keepdims=True)
    high, middle, low = thirds(d_gain)
    row = iota((16, width), 0)
    gain_rows = jnp.where(row == 0, high.astype(F32), 0.0)
    gain_rows = jnp.where(row == 1, middle.astype(F32), gain_rows)
    gain_rows = jnp.where(row == 2, low.astype(F32), gain_rows)
    grad_n = grad_h * gain[...].astype(F32)
    inner = jnp.mean(grad_n * normed, axis=-1, keepdims=True)
    d_res = cot[...].astype(F32) + inv_rms * (grad_n - normed * inner)
    out[0:tok, :] = d_res.astype(BF)
    out[tok : tok + 16, :] = gain_rows.astype(BF)
    gain_out[...] = d_res.astype(BF)


def combine_grads(routes, packed, mixed, gain, cot, n_exp):
    tok, width = cot.shape
    return call(
        functools.partial(combine_grads_body, n_exp),
        "combine_grads",
        (sds((tok + 16, width), BF), sds((tok, width), BF)),
        (1,),
        [whole(a.shape) for a in (routes, packed, mixed, gain, cot)],
        (whole((tok + 16, width)), whole((tok, width))),
        flops=2 * packed.shape[0] * 2 * tok * width,
        nbytes=8 * packed.shape[0] * width,
    )(routes, packed, mixed, gain, cot)


def combine_out_body(n_exp, routes, gates, packed, mixed, out):
    tok, width = mixed.shape
    quarter = width // 4
    spread, main, tails = pick_tokens(slot_table(routes[...], n_exp))
    parts = thirds(gate_table(routes[...], gates[...], n_exp))
    gate = (mm(parts[0], spread) + mm(parts[1], spread)) + mm(parts[2], spread)
    high = gate.astype(BF)
    low = (gate - high.astype(F32)).astype(BF)
    none = jnp.zeros_like(high)
    last = jnp.zeros((tok, quarter), F32)
    for c in range(PACK):
        pick = jnp.concatenate(
            [
                jnp.where(main, high, none),
                jnp.where(main, low, none),
                jnp.where(tails[c], high, none),
                jnp.where(tails[c], low, none),
            ],
            axis=0,
        )
        both = mm(pick, packed[:, c * quarter : (c + 1) * quarter])
        at = slice(c * quarter, (c + 1) * quarter)
        head = both[:tok] + both[tok : 2 * tok]
        out[:, at] = (mixed[:, at].astype(F32) + head).astype(BF)
        last = last + (both[2 * tok : 3 * tok] + both[3 * tok :])
    at = slice(PACK * quarter, width)
    out[:, at] = (mixed[:, at].astype(F32) + last).astype(BF)


def combine_out(routes, gates, packed, mixed, n_exp):
    tok, width = mixed.shape
    return call(
        functools.partial(combine_out_body, n_exp),
        "combine_out",
        sds((tok, width), BF),
        (1,),
        [whole(a.shape) for a in (routes, gates, packed, mixed)],
        whole((tok, width)),
        flops=2 * packed.shape[0] * 4 * tok * width,
        nbytes=6 * packed.shape[0] * width,
    )(routes, gates, packed, mixed)


SUB = 256


def unpack_rows(packed, quarter):
    perm = block_perm(SUB)
    return jnp.concatenate(
        [
            unpack(packed[j * SUB : (j + 1) * SUB, :], perm, quarter)
            for j in range(packed.shape[0] // SUB)
        ],
        axis=0,
    )


def repack_rows(rows, out, quarter):
    perm = block_perm(SUB)
    real = SUB * SLOTS // GROUP
    for j in range(rows.shape[0] // real):
        out[j * SUB : (j + 1) * SUB, :] = repack(rows[j * real : (j + 1) * real, :], perm, quarter)


def grad_act_body(packed, weight_out, rows_out, grad_act):
    quarter = weight_out.shape[1] // 4
    rows = unpack_rows(packed, quarter)
    rows_out[...] = rows
    grad_act[...] = mm(rows, weight_out[...], 1, 1)


def grad_act_call(packed, weight_out):
    hidden, width = weight_out.shape
    steps = 2
    block = packed.shape[0] // steps
    real = block * SLOTS // GROUP
    at = lambda i: (i, 0)
    return call(
        grad_act_body,
        "grad_act",
        (sds((real * steps, width), BF), sds((real * steps, hidden), F32)),
        (steps,),
        [pl.BlockSpec((block, packed.shape[1]), at), whole(weight_out.shape)],
        (pl.BlockSpec((real, width), at), pl.BlockSpec((real, hidden), at)),
        flops=2 * real * steps * hidden * width,
        nbytes=2 * hidden * width + 10 * real * steps * width,
    )(packed, weight_out)


def expert_body(packed, weight_in, grad_act_ref, rows_out, act_out, ggu_out, packed_out):
    width, both = weight_in.shape
    hidden = both // 2
    quarter = width // 4
    rows = unpack_rows(packed, quarter)
    rows_out[...] = rows
    gate_part = mm(rows, weight_in[:, :hidden])
    up_part = mm(rows, weight_in[:, hidden:])
    grad_act = grad_act_ref[...]
    sigma = jax.nn.sigmoid(gate_part)
    silu = gate_part * sigma
    act_out[...] = (silu * up_part).astype(BF)
    grad_gate = (grad_act * up_part * sigma * (1.0 + gate_part * (1.0 - sigma))).astype(BF)
    grad_up = (grad_act * silu).astype(BF)
    ggu_out[:, :hidden] = grad_gate
    ggu_out[:, hidden:] = grad_up
    back = mm(jnp.concatenate([grad_gate, grad_up], axis=1), weight_in[...], 1, 1).astype(BF)
    repack_rows(back, packed_out, quarter)


def expert_call(packed, weight_in, grad_act):
    width, both = weight_in.shape
    hidden = both // 2
    steps = 2
    block = packed.shape[0] // steps
    real = block * SLOTS // GROUP
    at = lambda i: (i, 0)
    return call(
        expert_body,
        "expert",
        (
            sds((real * steps, width), BF),
            sds((real * steps, hidden), BF),
            sds((real * steps, both), BF),
            sds(packed.shape, BF),
        ),
        (steps,),
        [
            pl.BlockSpec((block, packed.shape[1]), at),
            whole(weight_in.shape),
            pl.BlockSpec((real, hidden), at),
        ],
        (
            pl.BlockSpec((real, width), at),
            pl.BlockSpec((real, hidden), at),
            pl.BlockSpec((real, both), at),
            pl.BlockSpec((block, packed.shape[1]), at),
        ),
        flops=4 * real * steps * both * width,
        nbytes=2 * both * width + 10 * real * steps * width,
    )(packed, weight_in, grad_act)


def expert_y_body(act, weight_out, packed_out):
    rows = mm(act[...], weight_out[...]).astype(BF)
    repack_rows(rows, packed_out, weight_out.shape[1] // 4)


def expert_y_call(act, weight_out):
    hidden, width = weight_out.shape
    steps = 2
    real = act.shape[0] // steps
    block = real * GROUP // SLOTS
    at = lambda i: (i, 0)
    return call(
        expert_y_body,
        "expert_y",
        sds((block * steps, width * 3 // 4), BF),
        (steps,),
        [pl.BlockSpec((real, hidden), at), whole(weight_out.shape)],
        pl.BlockSpec((block, width * 3 // 4), at),
        flops=2 * real * steps * hidden * width,
        nbytes=2 * hidden * width + 4 * real * steps * width,
    )(act, weight_out)


def project_body(ctx_own, ctx_got, w_own, w_got, out):
    out[0] = (mm(ctx_own[0], w_own[...]) + mm(ctx_got[0], w_got[...])).astype(BF)


def project(ctx_own, ctx_got, w_own, w_got):
    blocks, tok, cols = ctx_own.shape
    width = w_own.shape[1]
    at = lambda i: (i, 0, 0)
    return call(
        project_body,
        "project",
        sds((blocks, tok, width), BF),
        (blocks,),
        [
            pl.BlockSpec((1, tok, cols), at),
            pl.BlockSpec((1, tok, cols), at),
            whole(w_own.shape),
            whole(w_got.shape),
        ],
        pl.BlockSpec((1, tok, width), at),
        flops=4 * blocks * tok * cols * width,
        nbytes=4 * blocks * tok * (cols + width),
    )(ctx_own, ctx_got, w_own, w_got)


def trade(values):
    n_all = lax.axis_size("ctx") * lax.axis_size("tp")
    shaped = values.reshape(n_all, GROUP, values.shape[1])
    moved = lax.all_to_all(shaped, ("ctx", "tp"), split_axis=0, concat_axis=0, tiled=True)
    return moved.reshape(values.shape)


def on_device(
    context, residual, o_weight, norm_gain, routes, gate_weights, expert_in, expert_out, cotangent
):
    tok, width = residual.shape
    n_tp = lax.axis_size("tp")
    n_ctx = lax.axis_size("ctx")
    n_exp = n_tp * n_ctx
    chips = n_tp // 2
    cols = context.shape[1]
    core = lax.axis_index("tp") % 2
    swap = [(t, t ^ 1) for t in range(n_tp)]
    same_core = [[t for t in range(n_tp) if t % 2 == c] for c in range(2)]
    gain_row = norm_gain.reshape(1, width)

    by_core = context.reshape(chips, 2, tok, cols)
    ctx_own = lax.dynamic_index_in_dim(by_core, core, 1, keepdims=False)
    ctx_give = lax.dynamic_index_in_dim(by_core, 1 - core, 1, keepdims=False)
    w_got = lax.ppermute(o_weight, "tp", swap)
    ctx_got = lax.ppermute(ctx_give, "tp", swap)
    partial = project(ctx_own, ctx_got, o_weight, w_got)
    parts = lax.all_to_all(
        partial, "tp", split_axis=0, concat_axis=0, tiled=True, axis_index_groups=same_core
    )

    grads_in = trade(pack_grads(routes, gate_weights, cotangent, n_exp))
    packed_h, mixed = norm_pack(routes, parts, residual, gain_row, n_exp)
    h_in = trade(packed_h)

    weight_in, weight_out = expert_in[0], expert_out[0]
    grads, grad_act = grad_act_call(grads_in, weight_out)
    arrived, act, ggu, packed_back = expert_call(h_in, weight_in, grad_act)
    back = trade(packed_back)
    packed_y = expert_y_call(act, weight_out)
    y_back = trade(packed_y)
    d_expert_out = contract(act, grads, 0, 0).astype(BF)[None]
    d_expert_in = contract(arrived, ggu, 0, 0).astype(BF)[None]

    d_res_gain, d_residual = combine_grads(routes, back, mixed, gain_row, cotangent, n_exp)
    layer_out = combine_out(routes, gate_weights, y_back, mixed, n_exp)

    spread = jnp.broadcast_to(d_res_gain[None], (chips,) + d_res_gain.shape)
    got = lax.all_to_all(
        spread, "tp", split_axis=0, concat_axis=0, tiled=True, axis_index_groups=same_core
    )
    d_rows = got[:, :tok].reshape(chips * tok, width)
    d_gain_chip = jnp.sum(got[:, tok : tok + 3].astype(F32), axis=(0, 1))
    flat_own = ctx_own.reshape(chips * tok, cols)
    flat_got = ctx_got.reshape(chips * tok, cols)
    w_grad_give = contract(flat_got, d_rows, 0, 0).astype(BF)
    w_grad_got = lax.ppermute(w_grad_give, "tp", swap)
    ctx_grad_give = contract(d_rows, w_got, 1, 1).astype(BF)
    ctx_grad_got = lax.ppermute(ctx_grad_give, "tp", swap)
    w_grad = (contract(flat_own, d_rows, 0, 0) + w_grad_got.astype(F32)).astype(BF)
    ctx_grad = contract(d_rows, o_weight, 1, 1).astype(BF)

    gain_got = lax.ppermute(d_gain_chip, "tp", swap)
    gain_parts = jnp.stack(thirds(d_gain_chip + gain_got)).reshape(1, -1, cols)
    gain_parts = jnp.broadcast_to(gain_parts, (n_ctx,) + gain_parts.shape[1:])
    out_cols = width // n_ctx
    by_ctx = w_grad.reshape(cols, n_ctx, out_cols).transpose(1, 0, 2)
    sent = jnp.concatenate([by_ctx, gain_parts.reshape(n_ctx, -1, out_cols)], axis=1)
    final = lax.all_to_all(sent, "ctx", split_axis=0, concat_axis=0, tiled=True).astype(F32)
    d_o_weight = jnp.sum(final[:, :cols], axis=0)
    d_gain = jnp.sum(final[:, cols:].reshape(n_ctx * 3, width), axis=0)

    mine = ctx_grad.reshape(chips, 1, tok, cols)
    other = ctx_grad_got.reshape(chips, 1, tok, cols)
    d_context = jnp.where(
        core == 0,
        jnp.concatenate([mine, other], axis=1),
        jnp.concatenate([other, mine], axis=1),
    ).reshape(context.shape)
    return (layer_out, d_context, d_residual, d_o_weight, d_gain, d_expert_in, d_expert_out)


def solution(mesh):
    rows = P(("ctx", "tp"), None)
    experts = P(("ctx", "tp"), None, None)
    in_specs = (P("ctx", "tp"), rows, P("tp", None), P(), rows, rows, experts, experts, rows)
    out_specs = (rows, P("ctx", "tp"), rows, P("tp", "ctx"), P(), experts, experts)
    return jax.shard_map(
        on_device, mesh=mesh, in_specs=in_specs, out_specs=out_specs, check_vma=False
    )
```

time: 640 us -> 398 us (0.62); the launches traced: 629 us -> 396 us
  waiting for transfers between devices: 337 us -> 191 us
  local copies, waits for them, and re-layouts: 92.4 us -> 16.3 us
  Pallas kernels: 0 us -> 64.6 us
  matrix products: 63.6 us -> 25.5 us
  blocking collectives: 64.6 us -> 46.7 us
  other arithmetic: 22.8 us -> 6.08 us
  between operations: 14.5 us -> 0.9 us
  starting transfers between devices: 33.7 us -> 45.2 us
    reduce_scatter x2 -> x0, waiting for transfers between devices: 156 us -> none  [the longest x1 156 us: on_device(): lax.psum_scatter(jnp.dot(ctx_rows, o_weight, preferred_element_type=jnp.f...]
    all_to_all x4 -> x6, waiting for transfers between devices: 119 us -> 190 us  [the longest x3 78.7 us: trade(): lax.all_to_all(shaped, ('ctx', 'tp'), split_axis=0, concat_axis=0, tiled=...]
    psum x1 -> x0, blocking collectives: 64.6 us -> none  [on_device(): d_gain = lax.psum(jnp.sum(grad_h * normed, axis=0), ('ctx', 'tp'))]
    pallas_call x0 -> x8, Pallas kernels: none -> 64.6 us  [the longest x1 18.4 us: expert_call(): call(expert_body, 'expert', (sds((real * steps, width), BF), sds((real *...]
    all_gather x1 -> x0, waiting for transfers between devices: 62.9 us -> none  [on_device(): shard_rows = lax.all_gather(d_residual, 'tp', axis=0, tiled=True)]
    reshape x9 -> x3, local copies, waits for them, and re-layouts: 51.8 us -> 0.71 us  [the longest x1 0.6 us: on_device(): gain_row = norm_gain.reshape(1, width)]
    all_to_all x0 -> x1, blocking collectives: none -> 46.7 us  [trade(): lax.all_to_all(shaped, ('ctx', 'tp'), split_axis=0, concat_axis=0, tiled=...]
    dot_general x9 -> x6, matrix products: 63.6 us -> 25.5 us  [mm(): lax.dot_general(a, b, (((da,), (db,)), ((), ())), preferred_element_type=...]
  transfers between devices with their start and end apart: 7 -> 11, of which waited for: 5 -> 7; matrix products, arithmetic and copies ran while one was open for 17% -> 10% of each run, Pallas kernels for 0% -> 8%
where the time goes in v1:
time: 398 us; the launch traced here: 396 us
  waiting for transfers between devices  191 us (48%)
  Pallas kernels  64.6 us (16%)
  blocking collectives  46.7 us (12%)
  starting transfers between devices  45.2 us (11%)
  matrix products  25.5 us (6%)
  local copies, waits for them, and re-layouts  16.3 us (4%)
  other arithmetic  6.08 us (2%)
    all_to_all x3, waiting for transfers between devices, trade(): lax.all_to_all(shaped, ('ctx', 'tp'), split_axis=0, concat_axis=0, tiled=...  78.7 us
    all_to_all x1, waiting for transfers between devices, on_device(): lax.all_to_all(spread, 'tp', split_axis=0, concat_axis=0, tiled=True, axi...  55.2 us
    all_to_all x1, waiting for transfers between devices, on_device(): lax.all_to_all(partial, 'tp', split_axis=0, concat_axis=0, tiled=True, ax...  51 us
    all_to_all x1, blocking collectives, trade(): lax.all_to_all(shaped, ('ctx', 'tp'), split_axis=0, concat_axis=0, tiled=...  46.7 us
    all_to_all x3, starting transfers between devices, trade(): lax.all_to_all(shaped, ('ctx', 'tp'), split_axis=0, concat_axis=0, tiled=...  26.2 us
    dot_general x6, matrix products, mm(): lax.dot_general(a, b, (((da,), (db,)), ((), ())), preferred_element_type=...  25.5 us
    pallas_call x1, Pallas kernels, expert_call(): call(expert_body, 'expert', (sds((real * steps, width), BF), sds((real *...  18.4 us
    all_to_all x1, starting transfers between devices, on_device(): lax.all_to_all(partial, 'tp', split_axis=0, concat_axis=0, tiled=True, ax...  8.3 us
  transfers between devices with their start and end apart: 11, of which 7 were waited for; matrix products, arithmetic and copies ran while one was open for 10% of the time, Pallas kernels for 8%

profile of v1, /device:TPU:2, one launch (start us, length us, event | category | flops | bytes accessed | tf_op | source)
XLA Modules:
  0.0 396.5 jit_solution(4236233087145009109)
XLA Ops:
  0.7 2.1 dynamic-slice_bitcast_fusion
  2.8 0.5 collective-permute-start
  3.3 1.5 collective-permute-done.ctx_got
  4.8 0.8 copy-done.10
  5.6 0.3 copy-done.9
  6.0 8.1 %project.1 = bf16[8,128,2048]{2,1,0:T(8,128)(2,1)} custom-call(bf16[8,128,256]{2,1,0:T(8,128)(2,1)} %bitcast.66, bf16[8,128,256]{2,1,0:T(8,128)(2,1)} %copy-done.10, bf16[256,2048]{1,0:T(8,128)(2,1)} %w_own.1, bf16[256,2048]{1,0:T(8,128)(2,1)} %copy-done.9), custom_call_target="tpu_custom_call" | custom-call | flops 2147483648 | bytes 9437184 | tf_op jit(solution)/shard_map/project/pallas_call | solution.py:447
  14.0 8.3 %all-to-all-start = ((bf16[8,128,2048]{2,1,0:T(8,128)(2,1)}), bf16[8,128,2048]{2,1,0:T(8,128)(2,1)}, u32[]{:S(2)}, u32[]{:S(2)}) async-start(bf16[8,128,2048]{2,1,0:T(8,128)(2,1)} %project.1), calls=%async_computation | async-start | bytes 8388608 | tf_op jit(solution)/shard_map/all_to_all | solution.py:491
  22.4 0.7 copy.31.routes
  23.1 0.7 copy.32.gates
  23.8 4.9 %pack_grads.1 = bf16[1024,1536]{1,0:T(8,128)(2,1)} custom-call(s32[128,4]{1,0:T(8,128)} %copy.31.routes, f32[128,4]{1,0:T(8,128)} %copy.32.gates, bf16[128,2048]{1,0:T(8,128)(2,1)} %cot.3), custom_call_target="tpu_custom_call" | custom-call | flops 1073741824 | bytes 16777216 | tf_op jit(solution)/shard_map/pack_grads/pallas_call | solution.py:161
  28.8 51.0 %all-to-all-done.parts = bf16[8,128,2048]{2,1,0:T(8,128)(2,1)} async-done(((bf16[8,128,2048]{2,1,0:T(8,128)(2,1)}), bf16[8,128,2048]{2,1,0:T(8,128)(2,1)}, u32[]{:S(2)}, u32[]{:S(2)}) %all-to-all-start) | async-done | bytes 4194336 | tf_op jit(solution)/shard_map/all_to_all | solution.py:491
  79.8 10.4 %all-to-all-start.2 = ((bf16[128,8,1536]{2,1,0:T(8,128)(2,1)}), bf16[128,8,1536]{2,1,0:T(8,128)(2,1)S(1)}, u32[]{:S(2)}, u32[]{:S(2)}) async-start(bf16[128,8,1536]{2,1,0:T(8,128)(2,1)} %bitcast.60), calls=%async_computation.2 | async-start | bytes 6291456 | tf_op jit(solution)/shard_map/all_to_all | solution.py:467
  90.2 0.6 reshape.73.gain
  90.8 7.2 %norm_pack.1 = (bf16[1024,1536]{1,0:T(8,128)(2,1)}, bf16[128,2048]{1,0:T(8,128)(2,1)}) custom-call(s32[128,4]{1,0:T(8,128)} %copy.31.routes, bf16[8,128,2048]{2,1,0:T(8,128)(2,1)} %all-to-all-done.parts, bf16[128,2048]{1,0:T(8,128)(2,1)} %residual.1, bf16[1,2048]{1,0:T(2,128)(2,1)} %reshape.73.gain), custom_call_target="tpu_custom_call" | custom-call | flops 1073741824 | bytes 33554432 | tf_op jit(solution)/shard_map/norm_pack/pallas_call | solution.py:208
  98.0 33.0 %all-to-all-done.2 = bf16[128,8,1536]{2,1,0:T(8,128)(2,1)S(1)} async-done(((bf16[128,8,1536]{2,1,0:T(8,128)(2,1)}), bf16[128,8,1536]{2,1,0:T(8,128)(2,1)S(1)}, u32[]{:S(2)}, u32[]{:S(2)}) %all-to-all-start.2) | async-done | bytes 3145760 | tf_op jit(solution)/shard_map/all_to_all | solution.py:467
  131.0 1.7 copy-done.3
  132.7 6.2 %all-to-all-start.1 = ((bf16[128,8,1536]{2,1,0:T(8,128)(2,1)}), bf16[128,8,1536]{2,1,0:T(8,128)(2,1)}, u32[]{:S(2)}, u32[]{:S(2)}) async-start(bf16[128,8,1536]{2,1,0:T(8,128)(2,1)} %bitcast.59), calls=%async_computation.1 | async-start | bytes 6291456 | tf_op jit(solution)/shard_map/all_to_all | solution.py:467
  138.8 7.6 %grad_act.1 = (bf16[768,2048]{1,0:T(8,128)(2,1)}, f32[768,768]{1,0:T(8,128)}) custom-call(bf16[1024,1536]{1,0:T(8,128)(2,1)} %bitcast.58, bf16[768,2048]{1,0:T(8,128)(2,1)} %bitcast.69), custom_call_target="tpu_custom_call" | custom-call | flops 2415919104 | bytes 18874368 | tf_op jit(solution)/shard_map/grad_act/pallas_call | solution.py:351
  146.4 32.9 %all-to-all-done.1 = bf16[128,8,1536]{2,1,0:T(8,128)(2,1)} async-done(((bf16[128,8,1536]{2,1,0:T(8,128)(2,1)}), bf16[128,8,1536]{2,1,0:T(8,128)(2,1)}, u32[]{:S(2)}, u32[]{:S(2)}) %all-to-all-start.1) | async-done | bytes 3145760 | tf_op jit(solution)/shard_map/all_to_all | solution.py:467
  179.3 18.4 %expert.1 = (bf16[768,2048]{1,0:T(8,128)(2,1)}, bf16[768,768]{1,0:T(8,128)(2,1)}, bf16[768,1536]{1,0:T(8,128)(2,1)}, bf16[1024,1536]{1,0:T(8,128)(2,1)}) custom-call(bf16[1024,1536]{1,0:T(8,128)(2,1)} %bitcast.4.packed, bf16[2048,1536]{1,0:T(8,128)(2,1)} %bitcast.68, f32[768,768]{1,0:T(8,128)} %get-tuple-element.18.grad_act_ref), custom_call_target="tpu_custom_call" | custom-call | flops 9663676416 | bytes 22020096 | tf_op jit(solution)/shard_map/expert/pallas_call | solution.py:390
  197.7 46.7 %all_to_all.35 = bf16[128,8,1536]{2,1,0:T(8,128)(2,1)} all-to-all(bf16[128,8,1536]{2,1,0:T(8,128)(2,1)} %bitcast.61), channel_id=1, replica_groups=mesh['ctx'=8,'tp'=16] {'ctx','tp'}, dimensions={0} | all-to-all | bytes 6291456 | tf_op jit(solution)/shard_map/all_to_all | solution.py:467
  244.4 5.0 %combine_grads.1 = (bf16[144,2048]{1,0:T(8,128)(2,1)}, bf16[128,2048]{1,0:T(8,128)(2,1)}) custom-call(s32[128,4]{1,0:T(8,128)} %copy.31.routes, bf16[1024,1536]{1,0:T(8,128)(2,1)} %bitcast.50, bf16[128,2048]{1,0:T(8,128)(2,1)} %get-tuple-element.20.mixed.mixed_ref, bf16[1,2048]{1,0:T(2,128)(2,1)} %reshape.73.gain, bf16[128,2048]{1,0:T(8,128)(2,1)} %cot.3), custom_call_target="tpu_custom_call" | custom-call | flops 1073741824 | bytes 16777216 | tf_op jit(solution)/shard_map/combine_grads/pallas_call | solution.py:262
  249.4 3.8 broadcast_in_dim.19
  253.2 5.6 %all-to-all-start.5 = ((bf16[8,144,2048]{2,1,0:T(8,128)(2,1)}), bf16[8,144,2048]{2,1,0:T(8,128)(2,1)}, u32[]{:S(2)}, u32[]{:S(2)}) async-start(bf16[8,144,2048]{2,1,0:T(8,128)(2,1)} %broadcast_in_dim.19), calls=%async_computation.5 | async-start | bytes 9437184 | tf_op jit(solution)/shard_map/all_to_all | solution.py:512
  258.9 7.9 %expert_y.1 = bf16[1024,1536]{1,0:T(8,128)(2,1)} custom-call(bf16[768,768]{1,0:T(8,128)(2,1)} %get-tuple-element.19.act, bf16[768,2048]{1,0:T(8,128)(2,1)} %bitcast.70), custom_call_target="tpu_custom_call" | custom-call | flops 2415919104 | bytes 9437184 | tf_op jit(solution)/shard_map/expert_y/pallas_call | solution.py:427
  266.8 55.2 %all-to-all-done.5 = bf16[8,144,2048]{2,1,0:T(8,128)(2,1)} async-done(((bf16[8,144,2048]{2,1,0:T(8,128)(2,1)}), bf16[8,144,2048]{2,1,0:T(8,128)(2,1)}, u32[]{:S(2)}, u32[]{:S(2)}) %all-to-all-start.5) | async-done | bytes 4718624 | tf_op jit(solution)/shard_map/all_to_all | solution.py:512
  322.0 9.7 %all-to-all-start.3 = ((bf16[128,8,1536]{2,1,0:T(8,128)(2,1)}), bf16[128,8,1536]{2,1,0:T(8,128)(2,1)S(1)}, u32[]{:S(2)}, u32[]{:S(2)}) async-start(bf16[128,8,1536]{2,1,0:T(8,128)(2,1)} %bitcast.57), calls=%async_computation.3 | async-start | bytes 6291456 | tf_op jit(solution)/shard_map/all_to_all | solution.py:467
  331.7 9.2 %fusion = bf16[1,2048,1536]{2,1,0:T(8,128)(2,1)} fusion(bf16[768,2048]{1,0:T(8,128)(2,1)} %get-tuple-element.24, bf16[768,1536]{1,0:T(8,128)(2,1)} %get-tuple-element.25), kind=kOutput, calls=%fused_computation.1 | convolution fusion | flops 4834983936 | bytes 11796480 | tf_op jit(solution)/shard_map/dot_general | solution.py:19
  340.9 4.6 %fusion.2 = bf16[256,2048]{1,0:T(8,128)(2,1)} fusion(bf16[8,128,256]{2,1,0:T(8,128)(2,1)S(1)} %copy-done.11, bf16[8,144,2048]{2,1,0:T(8,128)(2,1)} %all-to-all-done.5), kind=kOutput, calls=%fused_computation.5 | convolution fusion | flops 1074266112 | bytes 5767168 | tf_op jit(solution)/shard_map/dot_general | solution.py:19
  345.6 4.0 %fusion.1 = bf16[1,768,2048]{2,1,0:T(8,128)(2,1)} fusion(bf16[768,768]{1,0:T(8,128)(2,1)S(1)} %copy-done.12, bf16[768,2048]{1,0:T(8,128)(2,1)S(1)} %copy-done.13), kind=kOutput, calls=%fused_computation.3 | convolution fusion | flops 2417491968 | bytes 7471104 | tf_op jit(solution)/shard_map/dot_general | solution.py:19
  349.6 1.0 convert_reduce_fusion
  350.7 0.4 collective-permute-start.4
  351.1 2.5 slice.16
  353.6 2.6 fusion.5
  356.4 2.1 add_convert_fusion
  358.6 1.1 pad_maximum_fusion
  359.7 12.8 %all-to-all-done.3 = bf16[128,8,1536]{2,1,0:T(8,128)(2,1)S(1)} async-done(((bf16[128,8,1536]{2,1,0:T(8,128)(2,1)}), bf16[128,8,1536]{2,1,0:T(8,128)(2,1)S(1)}, u32[]{:S(2)}, u32[]{:S(2)}) %all-to-all-start.3) | async-done | bytes 3145760 | tf_op jit(solution)/shard_map/all_to_all | solution.py:467
  372.5 1.7 copy-done.2
  374.2 3.8 all-to-all-start.6
  378.0 3.8 convolution_convert_fusion.2
  381.8 5.5 %combine_out.1 = bf16[128,2048]{1,0:T(8,128)(2,1)} custom-call(s32[128,4]{1,0:T(8,128)} %copy.31.routes, f32[128,4]{1,0:T(8,128)} %copy.32.gates, bf16[1024,1536]{1,0:T(8,128)(2,1)} %bitcast.56, bf16[128,2048]{1,0:T(8,128)(2,1)} %get-tuple-element.20.mixed.mixed_ref), custom_call_target="tpu_custom_call" | custom-call | flops 2147483648 | bytes 12582912 | tf_op jit(solution)/shard_map/combine_out/pallas_call | solution.py:305
  387.4 1.3 convolution_convert_fusion.3
  388.7 0.2 maximum_select_fusion
  388.8 1.0 copy.34
  389.9 4.9 %all-to-all-done.6 = bf16[8,280,256]{2,1,0:T(8,128)(2,1)S(1)} async-done(((bf16[8,280,256]{2,1,0:T(8,128)(2,1)}), bf16[8,280,256]{2,1,0:T(8,128)(2,1)S(1)}, u32[]{:S(2)}, u32[]{:S(2)}) %all-to-all-start.6) | async-done | bytes 1146912 | tf_op jit(solution)/shard_map/all_to_all | solution.py:532
  394.8 0.2 convert_element_type.53
  395.0 0.8 slice_reduce_fusion
  395.9 0.6 reduce_sum.29
  (41 shorter events, 0.6 us)
Async XLA Ops:
  0.6 4.2 %collective-permute-start.1 = (bf16[256,2048]{1,0:T(8,128)(2,1)}, bf16[256,2048]{1,0:T(8,128)(2,1)S(1)}, u32[]{:S(2)}, u32[]{:S(2)}) collective-permute-start(bf16[256,2048]{1,0:T(8,128)(2,1)} %w_own.1), channel_id=1, source_target_pairs={{0,1},{1,0},{2,3},{3,2},{4,5},{5,4},{6,7},{7,6},{8,9},{9,8},{10,11... | collective-permute-start | bytes 3145736 | tf_op jit(solution)/shard_map/ppermute | solution.py:488
  2.8 2.0 collective-permute-start
  4.8 0.8 copy-start.10
  4.8 1.1 copy-start.9
  14.0 8.3 %copy-start.6 = (s32[128,4]{0,1:T(4,128)S(1)}, s32[128,4]{0,1:T(4,128)}, u32[]{:S(2)}) copy-start(s32[128,4]{0,1:T(4,128)} %param.13) | copy-start | bytes 6148
  14.0 9.1 %copy-start.7 = (f32[128,4]{0,1:T(4,128)S(1)}, f32[128,4]{0,1:T(4,128)}, u32[]{:S(2)}) copy-start(f32[128,4]{0,1:T(4,128)} %param.14) | copy-start | bytes 6148
  14.0 65.7 %all-to-all-start = ((bf16[8,128,2048]{2,1,0:T(8,128)(2,1)}), bf16[8,128,2048]{2,1,0:T(8,128)(2,1)}, u32[]{:S(2)}, u32[]{:S(2)}) async-start(bf16[8,128,2048]{2,1,0:T(8,128)(2,1)} %project.1), calls=%async_computation | async-start | bytes 8388608 | tf_op jit(solution)/shard_map/all_to_all | solution.py:491
  79.8 10.4 %copy-start.5 = (bf16[2048]{0:T(1024)(128)(2,1)S(1)}, bf16[2048]{0:T(1024)(128)(2,1)}, u32[]{:S(2)}) copy-start(bf16[2048]{0:T(1024)(128)(2,1)} %param.12) | copy-start | bytes 12292
  79.8 51.2 %all-to-all-start.2 = ((bf16[128,8,1536]{2,1,0:T(8,128)(2,1)}), bf16[128,8,1536]{2,1,0:T(8,128)(2,1)S(1)}, u32[]{:S(2)}, u32[]{:S(2)}) async-start(bf16[128,8,1536]{2,1,0:T(8,128)(2,1)} %bitcast.60), calls=%async_computation.2 | async-start | bytes 6291456 | tf_op jit(solution)/shard_map/all_to_all | solution.py:467
  131.0 1.7 copy-start.3
  132.7 46.7 %all-to-all-start.1 = ((bf16[128,8,1536]{2,1,0:T(8,128)(2,1)}), bf16[128,8,1536]{2,1,0:T(8,128)(2,1)}, u32[]{:S(2)}, u32[]{:S(2)}) async-start(bf16[128,8,1536]{2,1,0:T(8,128)(2,1)} %bitcast.59), calls=%async_computation.1 | async-start | bytes 6291456 | tf_op jit(solution)/shard_map/all_to_all | solution.py:467
  253.2 68.8 %all-to-all-start.5 = ((bf16[8,144,2048]{2,1,0:T(8,128)(2,1)}), bf16[8,144,2048]{2,1,0:T(8,128)(2,1)}, u32[]{:S(2)}, u32[]{:S(2)}) async-start(bf16[8,144,2048]{2,1,0:T(8,128)(2,1)} %broadcast_in_dim.19), calls=%async_computation.5 | async-start | bytes 9437184 | tf_op jit(solution)/shard_map/all_to_all | solution.py:512
  322.0 50.5 %all-to-all-start.3 = ((bf16[128,8,1536]{2,1,0:T(8,128)(2,1)}), bf16[128,8,1536]{2,1,0:T(8,128)(2,1)S(1)}, u32[]{:S(2)}, u32[]{:S(2)}) async-start(bf16[128,8,1536]{2,1,0:T(8,128)(2,1)} %bitcast.57), calls=%async_computation.3 | async-start | bytes 6291456 | tf_op jit(solution)/shard_map/all_to_all | solution.py:467
  331.7 9.2 %copy-start.11 = (bf16[8,128,256]{2,1,0:T(8,128)(2,1)S(1)}, bf16[8,128,256]{2,1,0:T(8,128)(2,1)}, u32[]{:S(2)}) copy-start(bf16[8,128,256]{2,1,0:T(8,128)(2,1)} %copy-done.10) | copy-start | bytes 1572868
  340.9 4.8 %copy-start.12 = (bf16[768,768]{1,0:T(8,128)(2,1)S(1)}, bf16[768,768]{1,0:T(8,128)(2,1)}, u32[]{:S(2)}) copy-start(bf16[768,768]{1,0:T(8,128)(2,1)} %get-tuple-element.19.act) | copy-start | bytes 3538948
  340.9 4.8 %copy-start.13 = (bf16[768,2048]{1,0:T(8,128)(2,1)S(1)}, bf16[768,2048]{1,0:T(8,128)(2,1)}, u32[]{:S(2)}) copy-start(bf16[768,2048]{1,0:T(8,128)(2,1)} %get-tuple-element.26) | copy-start | bytes 9437188
  345.5 10.9 %collective-permute-start.3 = (bf16[256,2048]{1,0:T(8,128)(2,1)}, bf16[256,2048]{1,0:T(8,128)(2,1)}, u32[]{:S(2)}, u32[]{:S(2)}) collective-permute-start(bf16[256,2048]{1,0:T(8,128)(2,1)} %fusion.2), channel_id=1, source_target_pairs={{0,1},{1,0},{2,3},{3,2},{4,5},{5,4},{6,7},{7,6},{8,9},{9,8},{10,11... | collective-permute-start | bytes 3145736 | tf_op jit(solution)/shard_map/ppermute | solution.py:520
  350.7 3.0 copy-start.4
  350.7 5.6 %collective-permute-start.4 = (f32[2048]{0:T(1024)S(1)}, f32[2048]{0:T(1024)S(1)}, u32[]{:S(2)}, u32[]{:S(2)}) collective-permute-start(f32[2048]{0:T(1024)S(1)} %convert_reduce_fusion), channel_id=1, source_target_pairs={{0,1},{1,0},{2,3},{3,2},{4,5},{5,4},{6,7},{7,6},{8,9},{9,8},{10,11... | collective-permute-start | bytes 24584 | tf_op jit(solution)/shard_map/ppermute | solution.py:526
  353.6 2.6 copy-start
  372.5 1.7 copy-start.2
  374.2 20.6 %all-to-all-start.6 = ((bf16[8,280,256]{2,1,0:T(8,128)(2,1)}), bf16[8,280,256]{2,1,0:T(8,128)(2,1)S(1)}, u32[]{:S(2)}, u32[]{:S(2)}) async-start(bf16[8,280,256]{2,1,0:T(8,128)(2,1)} %pad_maximum_fusion), calls=%async_computation.6 | async-start | bytes 2293760 | tf_op jit(solution)/shard_map/all_to_all | solution.py:532
  381.7 6.9 %collective-permute-start.2 = (bf16[1024,256]{1,0:T(8,128)(2,1)S(1)}, bf16[1024,256]{1,0:T(8,128)(2,1)S(1)}, u32[]{:S(2)}, u32[]{:S(2)}) collective-permute-start(bf16[1024,256]{1,0:T(8,128)(2,1)S(1)} %convolution_convert_fusion.2), channel_id=1, source_target_pairs={{0,1},{1,0},{2,3},{3,2},{4,5},{5,4},{6,7},{7,6},{8,9},{9,8},{10,11... | collective-permute-start | bytes 1572872 | tf_op jit(solution)/shard_map/ppermute | solution.py:522
  381.8 5.5 %copy-start.1 = (bf16[8,128,2048]{2,1,0:T(8,128)(2,1)S(1)}, bf16[8,128,2048]{2,1,0:T(8,128)(2,1)}, u32[]{:S(2)}) copy-start(bf16[8,128,2048]{2,1,0:T(8,128)(2,1)} %copy-done) | copy-start | bytes 12582916
  381.8 5.5 %copy-start.8 = (bf16[256,2048]{1,0:T(8,128)(2,1)S(1)}, bf16[256,2048]{1,0:T(8,128)(2,1)}, u32[]{:S(2)}) copy-start(bf16[256,2048]{1,0:T(8,128)(2,1)} %w_own.1) | copy-start | bytes 3145732
